TPU v7x, 32 devices: a whole 2x2x4 slice. The times are simulated.
32 devices in a mesh: gx: 8 (over z, x), gy: 4 (over y, core).
Axes of the slice: x: 2, y: 2, z: 4, core: 2. Of those that a mesh axis runs over, the one named last changes fastest.
Arguments:
- innovations: float32 [2, 128, 16384], P(None, None, ('gx', 'gy')), may hold values from -18 to 18
- obs_column: int32 [16384], P(('gx', 'gy')), may hold values from 0 to 16383
- obs_scale: float32 [2, 128], replicated, may hold values from 0.25 to 4
- band_of_lat: int32 [512], P('gy'), may hold values from 0 to 7, as said below
- balance: bfloat16 [8, 2, 128, 128], replicated, may hold values from -0.3 to 1.5
- lon_filter: bfloat16 [2, 1024, 1024], replicated, may hold values from 0 to 1
- lat_filter: bfloat16 [2, 512, 512], replicated, may hold values from 0 to 1
Outputs:
- control: float32 [2, 128, 1024, 512], P(None, ('gx', 'gy'))
- increment: float32 [2, 128, 1024, 512], P(None, None, 'gx', 'gy')
Inputs may be any that keep to these rules, and one draw needn't show every extreme that they name: `obs_column`: column c of a tile lies at longitude offset c // 128 and latitude offset c % 128 within the tile. `band_of_lat`: never falls from one latitude to the next.
All inputs are finite; a program needn't handle non-finite values.
Results may differ from a plain program's by a relative error of at most 0.0049.
Values may be sent and summed in bfloat16 or wider, within the bound.
A program may use at most 192 MiB of HBM per device.

v0:
```python
import jax
import jax.numpy as jnp
from jax import lax
from jax.sharding import PartitionSpec as P

ITERS = 2


huber_edge = 1.5


def filter_adjoint(pieces, lon_tiled, lat_tiled):
    half_lon = jnp.einsum(
        "vaxj,vablxt->vbljt", lon_tiled, pieces, preferred_element_type=jnp.float32
    ).astype(jnp.bfloat16)
    return jnp.einsum("vbljt,vbtk->vljk", half_lon, lat_tiled, preferred_element_type=jnp.float32)


def filter_forward(planes, lon_tiled, lat_tiled):
    smooth_lon = jnp.einsum(
        "vaxj,vljk->vlaxk", lon_tiled, planes, preferred_element_type=jnp.float32
    ).astype(jnp.bfloat16)
    return jnp.einsum(
        "vlaxm,vbtm->vablxt", smooth_lon, lat_tiled, preferred_element_type=jnp.float32
    ).astype(jnp.bfloat16)


def shards(innovations, obs_column, obs_scale, band_of_lat, balance, lon_filter, lat_filter):
    lon_parts = lax.axis_size("gx")
    lat_parts = lax.axis_size("gy")
    devices = lon_parts * lat_parts
    var_count, levels, obs_count = innovations.shape
    lon_full = lon_filter.shape[1]
    lat_full = lat_filter.shape[1]
    lon_tile = lon_full // lon_parts
    lat_tile = lat_full // lat_parts
    columns = lon_tile * lat_tile
    per_dev = levels // devices
    lon_tiled = lon_filter.reshape(var_count, lon_parts, lon_tile, lon_full)
    lat_tiled = lat_filter.reshape(var_count, lat_parts, lat_tile, lat_full)
    inv_scale = obs_scale[:, :, None]
    one_hot = (
        band_of_lat[:, None] == jnp.arange(balance.shape[0], dtype=jnp.int32)[None, :]
    ).astype(jnp.bfloat16)
    balance_lat = jnp.einsum(
        "tb,bvlm->tvlm", one_hot, balance, preferred_element_type=jnp.float32
    ).astype(jnp.bfloat16)
    control = jnp.zeros((var_count, per_dev, lon_full, lat_full), jnp.float32)
    increment = jnp.zeros((var_count, levels, columns), jnp.float32)
    for iteration in range(ITERS):
        observed = jnp.take(increment, obs_column, axis=2)
        scaled = (observed - innovations) * inv_scale
        weighted = jnp.clip(scaled, -huber_edge, huber_edge) * inv_scale
        forcing = (
            jnp.zeros((var_count, levels, columns), jnp.float32).at[:, :, obs_column].add(weighted)
        )
        forcing = forcing.astype(jnp.bfloat16).reshape(var_count, levels, lon_tile, lat_tile)
        balanced = jnp.einsum(
            "tvlm,vlxt->vmxt", balance_lat, forcing, preferred_element_type=jnp.float32
        ).astype(jnp.bfloat16)
        pieces = lax.all_to_all(
            balanced.reshape(var_count, devices, per_dev, lon_tile, lat_tile),
            ("gx", "gy"),
            split_axis=1,
            concat_axis=1,
            tiled=True,
        )
        item_count = pieces.shape[2]
        tiled = pieces.reshape(var_count, lon_parts, lat_parts, item_count, lon_tile, lat_tile)
        adjoint = filter_adjoint(tiled, lon_tiled, lat_tiled)
        gradient = control + adjoint
        grad_local = jnp.sum(gradient * gradient)
        grad_norm = lax.psum(grad_local, ("gx", "gy"))
        smoothed = filter_forward(gradient.astype(jnp.bfloat16), lon_tiled, lat_tiled)
        outgoing = smoothed.reshape(var_count, devices, per_dev, lon_tile, lat_tile)
        returned = lax.all_to_all(outgoing, ("gx", "gy"), split_axis=1, concat_axis=1, tiled=True)
        returned = returned.reshape(var_count, levels, lon_tile, lat_tile)
        response = jnp.einsum(
            "tvlm,vmxt->vlxt", balance_lat, returned, preferred_element_type=jnp.float32
        )
        response = response.reshape(var_count, levels, columns)
        at_obs = jnp.take(response, obs_column, axis=2)
        weight = huber_edge / jnp.maximum(jnp.abs(scaled), huber_edge)
        curve_local = jnp.sum(weight * (inv_scale * at_obs) ** 2)
        curvature = lax.psum(curve_local, ("gx", "gy"))
        step_size = grad_norm / (grad_norm + curvature)
        control = control - step_size * gradient
        increment = increment - step_size * response
    return (control, increment.reshape(var_count, levels, lon_tile, lat_tile))


def solution(mesh):
    in_specs = (P(None, None, ("gx", "gy")), P(("gx", "gy")), P(), P("gy"), P(), P(), P())
    out_specs = (P(None, ("gx", "gy"), None, None), P(None, None, "gx", "gy"))
    return jax.shard_map(shards, mesh=mesh, in_specs=in_specs, out_specs=out_specs, check_vma=False)
```

profile of v0, /device:TPU:12, one launch (start us, length us, event | category | flops | bytes accessed | tf_op | source)
XLA Modules:
  0.0 1517.8 jit_solution(908462979379822091)
XLA Ops:
  0.6 0.8 compare_and_fusion
  1.4 0.7 compare_select_fusion
  2.1 6.6 convolution_convert_fusion
  8.8 12.6 copy.165
  21.4 6.1 broadcast.20
  27.5 7.2 gather_fusion
  35.3 6.1 broadcast.20.clone
  41.4 51.7 %scatter_fusion = f32[2,128,16384]{1,0,2:T(2,128)} fusion(f32[2,128,16384]{1,0,2:T(2,128)} %broadcast.20.clone, s32[512]{0:T(512)S(1)} %compare_select_fusion, f32[512,2,128]{2,1,0:T(2,128)S(1)} %copy.162), kind=kCustom, calls=%fused_computation.4 | custom fusion | flops 131072 | bytes 1574912 | tf_op jit(solution)/shard_map/scatter-add | solution.py:55
  93.1 7.3 convert_element_type.64
  100.4 14.7 fusion.69
  115.2 14.0 copy.166
  129.1 188.5 %all_to_all.20 = bf16[2,32,4,128,128]{4,3,2,0,1:T(8,128)(2,1)} all-to-all(bf16[2,32,4,128,128]{4,3,2,0,1:T(8,128)(2,1)} %copy.166), channel_id=1, replica_groups=mesh['gx'=8,'gy'=4] {'gx','gy'}, dimensions={1} | all-to-all | bytes 16777216 | tf_op jit(solution)/shard_map/all_to_all | solution.py:61
  317.6 21.4 %fusion = (f32[]{:T(128)}, f32[2,4,1024,512,1]{3,2,4,1,0:T(8,128)}) fusion(bf16[2,4,128,512,1]{3,2,1,4,0:T(8,128)(2,1)S(1)} %bitcast.190, bf16[2,8,128,1024,1,1]{3,2,1,4,5,0:T(8,128)(2,1)} %bitcast.207, bf16[2,8,4,4,128,128]{5,4,3,0,2,1:T(8,128)(2,1)} %bitcast.203), kind=kOutput, calls=%fused_computation.11 | convolution fusion | flops 12897484800 | bytes 30408708 | tf_op jit(solution)/shard_map/vbljt,vbtk->vljk/dot_general | solution.py:16
  339.0 22.1 %fusion.59 = bf16[2,4,8,128,4,128]{5,3,4,2,1,0:T(8,128)(2,1)} fusion(bf16[2,4,128,512,1,1]{3,2,1,5,4,0:T(8,128)(2,1)S(1)} %bitcast.192, bf16[2,8,128,1024,1]{3,2,1,4,0:T(8,128)(2,1)} %bitcast.208, f32[2,4,1024,512,1]{3,2,4,1,0:T(8,128)} %get-tuple-element.22), kind=kOutput, calls=%fused_computation.47 | convolution fusion | flops 12897484800 | bytes 30408704 | tf_op jit(solution)/shard_map/vlaxm,vbtm->vablxt/dot_general | solution.py:23
  361.1 10.3 copy.172
  371.5 187.7 %all_to_all.21 = bf16[2,32,4,128,128]{4,3,2,0,1:T(8,128)(2,1)} all-to-all(bf16[2,32,4,128,128]{4,3,2,0,1:T(8,128)(2,1)} %copy.172), channel_id=1, replica_groups=mesh['gx'=8,'gy'=4] {'gx','gy'}, dimensions={1} | all-to-all | bytes 16777216 | tf_op jit(solution)/shard_map/all_to_all | solution.py:76
  559.2 10.3 copy.173
  569.5 13.5 copy.174
  583.0 20.2 %fusion.53 = f32[2,128,128,128]{1,2,3,0:T(8,128)} fusion(bf16[2,128,128,128]{1,2,3,0:T(8,128)(2,1)} %copy.174, bf16[128,2,128,128]{3,0,2,1:T(8,128)(2,1)} %convolution_convert_fusion), kind=kOutput, calls=%fused_computation.45 | convolution fusion | flops 1073741824 | bytes 33554432 | tf_op jit(solution)/shard_map/tvlm,vmxt->vlxt/dot_general | solution.py:78
  603.1 15.5 %copy.176 = f32[2,128,128,128]{1,3,2,0:T(8,128)S(1)} copy(f32[2,128,128,128]{1,2,3,0:T(8,128)} %fusion.53) | data formatting | bytes 33554432 | tf_op jit(solution)/shard_map/tvlm,vmxt->vlxt/transpose | solution.py:78
  618.6 5.7 copy-done.1
  624.3 61.6 %copy.177 = f32[2,128,16384]{1,0,2:T(2,128)} copy(f32[2,128,16384]{1,2,0:T(8,128)S(1)} %bitcast.194) | data formatting | bytes 33554432 | tf_op jit(solution)/shard_map/reshape | solution.py:81
  685.9 7.2 gather_fusion.1
  693.4 1.0 fusion.81
  694.4 42.1 %all-reduce.1 = (f32[]{:T(128)}, f32[]{:T(128)}) all-reduce(f32[]{:T(128)} %get-tuple-element.21, f32[]{:T(128)} %fusion.81), channel_id=1, replica_groups=mesh['gx'=8,'gy'=4] {'gx','gy'}, use_global_device_ids=true, to_apply=%region_2.4 | all-reduce | flops 2 | bytes 16 | tf_op jit(solution)/shard_map/psum | solution.py:73
  738.4 29.2 %multiply_subtract_fusion.2 = f32[2,128,16384]{1,0,2:T(2,128)} fusion(f32[]{:T(128)S(6)} %div.13, f32[2,128,16384]{1,2,0:T(8,128)} %bitcast.195), kind=kLoop, calls=%fused_computation.17 | loop fusion | flops 8388608 | bytes 33554436 | tf_op jit(solution)/shard_map/sub | solution.py:88
  767.6 7.2 gather_fusion.2
  775.2 0.2 copy.181
  775.4 51.7 %scatter_fusion.1 = f32[2,128,16384]{1,0,2:T(2,128)} fusion(f32[2,128,16384]{1,0,2:T(2,128)} %broadcast.20, s32[512]{0:T(512)S(1)} %compare_select_fusion, f32[512,2,128]{2,1,0:T(2,128)S(1)} %copy.181), kind=kCustom, calls=%fused_computation.5 | custom fusion | flops 131072 | bytes 1574912 | tf_op jit(solution)/shard_map/scatter-add | solution.py:55
  827.1 7.3 convert_element_type.75
  834.4 14.7 fusion.72
  849.2 14.0 copy.184
  863.1 185.7 %all_to_all.22 = bf16[2,32,4,128,128]{4,3,2,0,1:T(8,128)(2,1)} all-to-all(bf16[2,32,4,128,128]{4,3,2,0,1:T(8,128)(2,1)} %copy.184), channel_id=1, replica_groups=mesh['gx'=8,'gy'=4] {'gx','gy'}, dimensions={1} | all-to-all | bytes 16777216 | tf_op jit(solution)/shard_map/all_to_all | solution.py:61
  1048.8 22.7 %multiply_reduce_fusion = (f32[]{:T(128)}, f32[2,4,1024,512]{3,2,1,0:T(8,128)}) fusion(bf16[2,4,128,512,1]{3,2,1,4,0:T(8,128)(2,1)S(1)} %bitcast.191, bf16[2,8,128,1024,1,1]{3,2,1,4,5,0:T(8,128)(2,1)} %bitcast.209, bf16[2,8,4,4,128,128]{5,4,3,0,2,1:T(8,128)(2,1)} %bitcast.204, f32[2,4,1024,512,1]{3,2,4,1,0:T(8,128)} %get-tuple-element.22, f32[]{:T(128)S(6)} %div.13), kind=kOutput, calls=%fused_computation.16 | convolution fusion | flops 12910067712 | bytes 47185928 | tf_op jit(solution)/shard_map/vbljt,vbtk->vljk/dot_general | solution.py:16
  1071.5 22.1 %fusion.64 = bf16[2,4,8,128,4,128]{5,3,4,2,1,0:T(8,128)(2,1)} fusion(bf16[2,4,128,512,1,1]{3,2,1,5,4,0:T(8,128)(2,1)S(1)} %bitcast.193, bf16[2,8,128,1024,1]{3,2,1,4,0:T(8,128)(2,1)} %bitcast.210, f32[2,4,1024,512]{3,2,1,0:T(8,128)} %get-tuple-element.24), kind=kOutput, calls=%fused_computation.48 | convolution fusion | flops 12897484800 | bytes 30408704 | tf_op jit(solution)/shard_map/vlaxm,vbtm->vablxt/dot_general | solution.py:23
  1093.6 10.3 copy.190
  1104.0 187.7 %all_to_all.23 = bf16[2,32,4,128,128]{4,3,2,0,1:T(8,128)(2,1)} all-to-all(bf16[2,32,4,128,128]{4,3,2,0,1:T(8,128)(2,1)} %copy.190), channel_id=1, replica_groups=mesh['gx'=8,'gy'=4] {'gx','gy'}, dimensions={1} | all-to-all | bytes 16777216 | tf_op jit(solution)/shard_map/all_to_all | solution.py:76
  1291.7 10.3 copy.191
  1302.0 13.5 copy.192
  1315.5 20.2 %fusion.56 = f32[2,128,128,128]{1,2,3,0:T(8,128)} fusion(bf16[2,128,128,128]{1,2,3,0:T(8,128)(2,1)} %copy.192, bf16[128,2,128,128]{3,0,2,1:T(8,128)(2,1)} %convolution_convert_fusion), kind=kOutput, calls=%fused_computation.46 | convolution fusion | flops 1073741824 | bytes 33554432 | tf_op jit(solution)/shard_map/tvlm,vmxt->vlxt/dot_general | solution.py:78
  1335.6 15.5 %copy.194 = f32[2,128,128,128]{1,3,2,0:T(8,128)S(1)} copy(f32[2,128,128,128]{1,2,3,0:T(8,128)} %fusion.56) | data formatting | bytes 33554432 | tf_op jit(solution)/shard_map/tvlm,vmxt->vlxt/transpose | solution.py:78
  1351.1 61.8 %copy.195 = f32[2,128,16384]{1,0,2:T(2,128)} copy(f32[2,128,16384]{1,2,0:T(8,128)S(1)} %bitcast.196) | data formatting | bytes 33554432 | tf_op jit(solution)/shard_map/reshape | solution.py:81
  1412.9 7.2 gather_fusion.3
  1420.4 1.0 fusion.77
  1421.4 42.0 %all-reduce = (f32[]{:T(128)}, f32[]{:T(128)}) all-reduce(f32[]{:T(128)} %get-tuple-element.23, f32[]{:T(128)} %fusion.77), channel_id=1, replica_groups=mesh['gx'=8,'gy'=4] {'gx','gy'}, use_global_device_ids=true, to_apply=%region_7.9 | all-reduce | flops 2 | bytes 16 | tf_op jit(solution)/shard_map/psum | solution.py:73
  1465.3 16.9 %multiply_subtract_fusion = f32[2,128,128,128]{1,2,3,0:T(8,128)} fusion(f32[2,128,128,128]{1,2,3,0:T(8,128)} %fusion.56, f32[2,128,128,128]{1,2,3,0:T(8,128)} %fusion.53, f32[]{:T(128)S(6)} %div.15, f32[]{:T(128)S(6)} %div.13), kind=kLoop, calls=%fused_computation.14 | loop fusion | flops 16777216 | bytes 50331656 | tf_op jit(solution)/shard_map/sub | solution.py:88
  1482.2 17.0 %multiply_subtract_fusion.1 = f32[2,4,1024,512]{3,2,1,0:T(8,128)} fusion(f32[2,4,1024,512]{3,2,1,0:T(8,128)} %get-tuple-element.24, f32[2,4,1024,512,1]{3,2,4,1,0:T(8,128)} %get-tuple-element.22, f32[]{:T(128)S(6)} %div.15, f32[]{:T(128)S(6)} %div.13), kind=kLoop, calls=%fused_computation.15 | loop fusion | flops 16777216 | bytes 50331656 | tf_op jit(solution)/shard_map/sub | solution.py:87
  1499.2 18.1 %copy.197 = f32[2,128,128,128]{3,2,1,0:T(8,128)} copy(f32[2,128,128,128]{1,2,3,0:T(8,128)} %multiply_subtract_fusion) | data formatting | bytes 33554432
  (15 shorter events, 1.3 us)
Async XLA Ops:
  0.6 317.0 %copy-start = (bf16[2,512,512]{2,1,0:T(8,128)(2,1)S(1)}, bf16[2,512,512]{2,1,0:T(8,128)(2,1)}, u32[]{:S(2)}) copy-start(bf16[2,512,512]{2,1,0:T(8,128)(2,1)} %param.15) | copy-start | bytes 3145732
  21.4 13.6 copy-start.2
  21.4 13.6 copy-start.3
  618.6 5.7 copy-start.1
where the time goes:
time: 1530 us; the launch traced here: 1520 us
  blocking collectives  834 us (55%)
  local copies, waits for them, and re-layouts  329 us (22%)
  other arithmetic  185 us (12%)
  matrix products  165 us (11%)
    all_to_all x2, blocking collectives, shards(): lax.all_to_all(outgoing, ('gx', 'gy'), split_axis=1, concat_axis=1, tiled...  375 us
    all_to_all x2, blocking collectives, shards(): lax.all_to_all(balanced.reshape(var_count, devices, per_dev, lon_tile, la...  374 us
    reshape x2, local copies, waits for them, and re-layouts, shards(): response = response.reshape(var_count, levels, columns)  123 us
    scatter-add x2, other arithmetic, shards(): jnp.zeros((var_count, levels, columns), jnp.float32).at[:, :, obs_column]  103 us
    psum x2, blocking collectives, shards(): grad_norm = lax.psum(grad_local, ('gx', 'gy'))  84 us
    sub x2, other arithmetic, shards(): increment = increment - step_size * response  46.1 us
    dot_general x2, matrix products, filter_forward(): jnp.einsum('vlaxm,vbtm->vablxt', smooth_lon, lat_tiled, preferred_element...  44.3 us
    dot_general x2, matrix products, filter_adjoint(): jnp.einsum('vbljt,vbtk->vljk', half_lon, lat_tiled, preferred_element_typ...  44.1 us

commit v1 on v0

v1 whole, which is shorter than its diff:
```python
import jax
import jax.numpy as jnp
from jax import lax
from jax.sharding import PartitionSpec as P

ITERS = 2


huber_edge = 1.5
AXES = ("gx", "gy")
f32 = jnp.float32
bf16 = jnp.bfloat16


def shards(innovations, obs_column, obs_scale, band_of_lat, balance, lon_filter, lat_filter):
    lon_parts = lax.axis_size("gx")
    lat_parts = lax.axis_size("gy")
    devices = lon_parts * lat_parts
    var_count, levels, obs_count = innovations.shape
    bands = balance.shape[0]
    lon_full = lon_filter.shape[1]
    lat_full = lat_filter.shape[1]
    lon_tile = lon_full // lon_parts
    lat_tile = lat_full // lat_parts
    per_dev = levels // devices
    lon_tiled = lon_filter.reshape(var_count, lon_parts, lon_tile, lon_full)
    lat_tiled = lat_filter.reshape(var_count, lat_parts, lat_tile, lat_full)
    inv_scale = obs_scale[:, :, None]
    band_ids = jnp.arange(bands, dtype=jnp.int32)
    band_hot = (band_of_lat[:, None] == band_ids[None, :]).astype(bf16)
    balance_lat = jnp.einsum("tb,bvlm->tvlm", band_hot, balance, preferred_element_type=f32).astype(
        bf16
    )

    own_lat = obs_column % lat_tile
    own_hot = own_lat[:, None] == jnp.arange(lat_tile, dtype=jnp.int32)[None, :]
    own_band = jnp.sum(jnp.where(own_hot, band_of_lat[None, :], 0), axis=1)
    in_band = (own_band[None, :] == band_ids[:, None]).astype(bf16)
    same = obs_column[:, None] == obs_column[None, :]
    order = jnp.arange(obs_count, dtype=jnp.int32)
    first = jnp.logical_not(jnp.any(same & (order[None, :] < order[:, None]), axis=1))
    same = same.astype(f32)

    sites = lax.all_gather(obs_column, AXES, tiled=True).reshape(lon_parts, lat_parts, obs_count)
    hot_lon = (
        (sites // lat_tile)[..., None] == jnp.arange(lon_tile, dtype=jnp.int32)
    ).astype(bf16)
    hot_lat = ((sites % lat_tile)[..., None] == jnp.arange(lat_tile, dtype=jnp.int32)).astype(bf16)

    def to_levels(values):
        return lax.all_to_all(
            values.reshape(var_count, devices, per_dev, -1), AXES, 1, 1, tiled=True
        )

    control = None
    total = None
    at_obs = None
    step_size = None
    for iteration in range(ITERS):
        if iteration == 0:
            observed = jnp.zeros_like(innovations)
        elif iteration == 1:
            observed = -step_size * at_obs
        else:
            observed = observed - step_size * at_obs
        scaled = (observed - innovations) * inv_scale
        weighted = jnp.clip(scaled, -huber_edge, huber_edge) * inv_scale
        forcing = jnp.einsum(
            "vlj,jk->vlk", weighted, same, precision=lax.Precision.HIGHEST
        ).astype(bf16)
        banded = forcing[None] * in_band[:, None, None, :]
        balanced = jnp.einsum("bvlm,bvlj->vmj", balance, banded, preferred_element_type=f32)
        balanced = jnp.where(first, balanced, 0.0).astype(bf16)
        pieces = to_levels(balanced).reshape(var_count, lon_parts, lat_parts, per_dev, obs_count)
        spread = jnp.einsum("vablj->abjvl", pieces)[..., None] * hot_lat[:, :, :, None, None, :]
        grid = jnp.einsum("abjx,abjvlt->abxvlt", hot_lon, spread, preferred_element_type=f32).astype(
            bf16
        )
        half_lon = jnp.einsum(
            "vaxj,abxvlt->vbljt", lon_tiled, grid, preferred_element_type=f32
        ).astype(bf16)
        adjoint = jnp.einsum("vbljt,vbtk->vljk", half_lon, lat_tiled, preferred_element_type=f32)
        gradient = adjoint if control is None else control + adjoint
        grad_local = jnp.sum(gradient * gradient)
        smooth_lon = jnp.einsum(
            "vaxj,vljk->vlaxk", lon_tiled, gradient.astype(bf16), preferred_element_type=f32
        ).astype(bf16)
        smoothed = jnp.einsum(
            "vlaxm,vbtm->vablxt", smooth_lon, lat_tiled, preferred_element_type=f32
        ).astype(bf16)
        rows = jnp.einsum("abjx,vablxt->abjvlt", hot_lon, smoothed, preferred_element_type=f32)
        rows = rows.astype(bf16) * hot_lat[:, :, :, None, None, :]
        picked = jnp.sum(rows.astype(f32), axis=-1).astype(bf16)
        picked = jnp.einsum("abjvl->vablj", picked).reshape(var_count, devices, per_dev, obs_count)
        seen = lax.all_to_all(picked, AXES, 1, 1, tiled=True)
        seen = seen.reshape(var_count, levels, obs_count)
        seen = seen[None] * in_band[:, None, None, :]
        at_obs = jnp.einsum("bvlm,bvmj->vlj", balance, seen, preferred_element_type=f32)
        weight = huber_edge / jnp.maximum(jnp.abs(scaled), huber_edge)
        curve_local = jnp.sum(weight * (inv_scale * at_obs) ** 2)
        sums = lax.psum(jnp.stack([grad_local, curve_local]), AXES)
        grad_norm = sums[0]
        step_size = grad_norm / (grad_norm + sums[1])
        moved = -step_size * gradient
        control = moved if control is None else control + moved
        moved = -step_size * smoothed.astype(f32)
        total = moved if total is None else total + moved
    outgoing = total.astype(bf16).reshape(var_count, devices, per_dev, lon_tile, lat_tile)
    returned = lax.all_to_all(outgoing, AXES, split_axis=1, concat_axis=1, tiled=True)
    returned = returned.reshape(var_count, levels, lon_tile, lat_tile)
    increment = jnp.einsum("tvlm,vmxt->vlxt", balance_lat, returned, preferred_element_type=f32)
    return (control, increment)


def solution(mesh):
    in_specs = (P(None, None, AXES), P(AXES), P(), P("gy"), P(), P(), P())
    out_specs = (P(None, AXES, None, None), P(None, None, "gx", "gy"))
    return jax.shard_map(shards, mesh=mesh, in_specs=in_specs, out_specs=out_specs, check_vma=False)
```

time: 1530 us -> 635 us (0.42)
  blocking collectives: 834 us -> 160 us
  local copies, waits for them, and re-layouts: 329 us -> 57.5 us
  waiting for transfers between devices: 0 us -> 158 us
  other arithmetic: 185 us -> 37.7 us
  matrix products: 165 us -> 195 us
    all_to_all x4 -> x3, blocking collectives: 750 us -> 43.2 us  [the longest x2 31.4 us: shards(): seen = lax.all_to_all(picked, AXES, 1, 1, tiled=True)]
    reshape x6 -> x8, local copies, waits for them, and re-layouts: 172 us -> 11.8 us  [the longest x1 10.3 us: shards(): total.astype(bf16).reshape(var_count, devices, per_dev, lon_tile, lat_tile)]
    all_to_all x0 -> x2, waiting for transfers between devices: none -> 158 us  [the longest x1 158 us: shards(): lax.all_to_all(outgoing, AXES, split_axis=1, concat_axis=1, tiled=True)]
    scatter-add x2 -> x0, other arithmetic: 103 us -> none  [shards(): jnp.zeros((var_count, levels, columns), jnp.float32).at[:, :, obs_column]]
    sub x3 -> x0, other arithmetic: 63.1 us -> none  [the longest x2 46.1 us: shards(): increment = increment - step_size * response]
    dot_general x7 -> x17, matrix products: 124 us -> 175 us  [the longest x2 44.6 us: shards(): jnp.einsum('vlaxm,vbtm->vablxt', smooth_lon, lat_tiled, preferred_element...]
    all_gather x0 -> x1, blocking collectives: none -> 33.4 us  [shards(): lax.all_gather(obs_column, AXES, tiled=True)]
    transpose x2 -> x0, local copies, waits for them, and re-layouts: 30.9 us -> none  [shards(): jnp.einsum('tvlm,vmxt->vlxt', balance_lat, returned, preferred_element_ty...]
  transfers between devices with their start and end apart: 0 -> 2, of which waited for: 0 -> 1; matrix products, arithmetic and copies ran while one was open for 0% -> 4% of each run, Pallas kernels for 0% -> 0%
where the time goes in v1:
time: 635 us; the launch traced here: 623 us
  matrix products  195 us (31%)
  blocking collectives  160 us (25%)
  waiting for transfers between devices  158 us (25%)
  local copies, waits for them, and re-layouts  57.5 us (9%)
  other arithmetic  37.7 us (6%)
  starting transfers between devices  9.61 us (2%)
    all_to_all x1, waiting for transfers between devices, shards(): lax.all_to_all(outgoing, AXES, split_axis=1, concat_axis=1, tiled=True)  158 us
    psum x2, blocking collectives, shards(): sums = lax.psum(jnp.stack([grad_local, curve_local]), AXES)  82.9 us
    dot_general x2, matrix products, shards(): jnp.einsum('vlaxm,vbtm->vablxt', smooth_lon, lat_tiled, preferred_element...  44.6 us
    dot_general x2, matrix products, shards(): jnp.einsum('vaxj,abxvlt->vbljt', lon_tiled, grid, preferred_element_type=...  36.9 us
    all_gather x1, blocking collectives, shards(): lax.all_gather(obs_column, AXES, tiled=True)  33.4 us
    all_to_all x2, blocking collectives, shards(): seen = lax.all_to_all(picked, AXES, 1, 1, tiled=True)  31.4 us
    dot_general x2, matrix products, shards(): jnp.einsum('vbljt,vbtk->vljk', half_lon, lat_tiled, preferred_element_typ...  27.5 us
    dot_general x2, matrix products, shards(): jnp.einsum('abjx,abjvlt->abxvlt', hot_lon, spread, preferred_element_type...  27.4 us
  transfers between devices with their start and end apart: 2, of which 1 were waited for; matrix products, arithmetic and copies ran while one was open for 4% of the time, Pallas kernels for 0%

profile of v1, /device:TPU:12, one launch (start us, length us, event | category | flops | bytes accessed | tf_op | source)
XLA Modules:
  0.0 622.7 jit_solution(17646267603712663744)
XLA Ops:
  0.6 0.8 add_select_fusion.2
  1.4 1.0 fusion.144
  2.4 1.2 copy.78
  3.7 1.6 convolution_convert_fusion.2
  5.3 0.2 copy.80
  5.4 0.9 select_reduce_fusion
  6.3 2.3 fusion.130
  8.7 0.8 copy.83
  9.5 6.0 all-to-all-start
  15.5 33.4 %all-gather = s32[32,1,512]{2,1,0:T(1,128)S(1)} all-gather(s32[1,1,512]{2,1,0:T(1,128)} %bitcast.246), channel_id=1, replica_groups=mesh['gx'=8,'gy'=4] {'gx','gy'}, dimensions={0}, use_global_device_ids=true | all-gather | bytes 67584 | tf_op jit(solution)/shard_map/all_gather | solution.py:44
  49.2 3.7 fusion.48
  52.9 13.7 %fusion.215 = bf16[8,4,128,2,4,128]{5,2,4,3,1,0:T(8,128)(2,1)} fusion(bf16[8,4,512,128]{2,3,1,0:T(8,128)(2,1)} %fusion.48, bf16[8,4,512,2,4]{2,4,3,1,0:T(4,128)(2,1)S(1)} %bitcast.242, s32[8,4,512]{2,1,0:T(4,128)S(1)} %get-tuple-element.10), kind=kOutput, calls=%fused_computation.46.clone.1 | convolution fusion | flops 4370464768 | bytes 12910592 | tf_op jit(solution)/shard_map/abjx,abjvlt->abxvlt/dot_general | solution.py:76
  66.6 18.4 %fusion.42 = bf16[2,4,4,128,1024,1]{4,3,2,0,1,5:T(8,128)(2,1)} fusion(bf16[2,8,128,1024,1,1]{3,2,1,0,5,4:T(8,128)(2,1)S(1)} %bitcast.249, bf16[8,4,128,2,4,128]{5,2,4,3,1,0:T(8,128)(2,1)} %fusion.215), kind=kOutput, calls=%fused_computation.45 | convolution fusion | flops 8589934592 | bytes 20971520 | tf_op jit(solution)/shard_map/vaxj,abxvlt->vbljt/dot_general | solution.py:79
  85.0 12.0 %fusion.4 = (f32[]{:T(128)}, f32[2,4,1024,512,1]{3,2,4,1,0:T(8,128)}) fusion(bf16[2,4,128,512,1]{3,2,1,4,0:T(8,128)(2,1)S(1)} %bitcast.234, bf16[2,4,4,128,1024,1]{4,3,2,0,1,5:T(8,128)(2,1)} %fusion.42), kind=kOutput, calls=%fused_computation.11 | convolution fusion | flops 4303355904 | bytes 26214404 | tf_op jit(solution)/shard_map/vbljt,vbtk->vljk/dot_general | solution.py:82
  97.1 22.4 %convert_bitcast_fusion.1 = bf16[2,8,4,4,128,128]{5,4,2,1,3,0:T(8,128)(2,1)} fusion(bf16[2,4,128,512,1,1]{3,2,1,5,4,0:T(8,128)(2,1)S(1)} %bitcast.236, bf16[2,8,128,1024,1]{3,2,1,4,0:T(8,128)(2,1)} %bitcast.247, f32[2,4,1024,512,1]{3,2,4,1,0:T(8,128)} %get-tuple-element.19), kind=kOutput, calls=%fused_computation.43 | convolution fusion | flops 12897484800 | bytes 30408704 | tf_op jit(solution)/shard_map/vlaxm,vbtm->vablxt/dot_general | solution.py:88
  119.4 12.1 %multiply_reduce_fusion.1 = bf16[8,4,512,2,4]{2,4,3,1,0:T(4,128)(2,1)S(1)} fusion(bf16[8,4,512,128]{2,3,1,0:T(8,128)(2,1)} %fusion.48, bf16[2,8,4,4,128,128]{5,4,2,1,3,0:T(8,128)(2,1)} %convert_bitcast_fusion.1, s32[8,4,512]{2,1,0:T(4,128)S(1)} %get-tuple-element.10), kind=kOutput, calls=%fused_computation.3 | convolution fusion | flops 4347265024 | bytes 12910592 | tf_op jit(solution)/shard_map/abjx,vablxt->abjvlt/dot_general | solution.py:91
  131.6 0.2 copy.92
  131.8 18.6 %all_to_all.25 = bf16[2,32,4,512]{3,0,2,1:T(2,128)(2,1)S(1)} all-to-all(bf16[2,32,4,512]{3,0,2,1:T(2,128)(2,1)S(1)} %copy.92), channel_id=1, replica_groups=mesh['gx'=8,'gy'=4] {'gx','gy'}, dimensions={1} | all-to-all | bytes 524288 | tf_op jit(solution)/shard_map/all_to_all | solution.py:95
  150.4 0.2 copy.93
  150.7 1.4 fusion.149
  152.1 1.3 pad_maximum_fusion
  153.4 41.4 %psum.14 = f32[2]{0:T(128)S(1)} all-reduce(f32[2]{0:T(128)S(1)} %pad_maximum_fusion), channel_id=1, replica_groups=mesh['gx'=8,'gy'=4] {'gx','gy'}, use_global_device_ids=true, to_apply=%region_5.6 | all-reduce | flops 2 | bytes 16 | tf_op jit(solution)/shard_map/psum | solution.py:101
  194.7 0.6 fusion.183
  197.1 0.8 convolution_convert_fusion.1
  198.1 1.5 fusion.133
  199.8 11.8 %all_to_all.26 = bf16[2,32,4,512]{3,2,0,1:T(4,128)(2,1)S(1)} all-to-all(bf16[2,32,4,512]{3,2,0,1:T(4,128)(2,1)S(1)} %copy.100), channel_id=1, replica_groups=mesh['gx'=8,'gy'=4] {'gx','gy'}, dimensions={1} | all-to-all | bytes 524288 | tf_op jit(solution)/shard_map/all_to_all | solution.py:51
  211.5 13.7 %fusion.211 = bf16[8,4,128,2,4,128]{5,2,4,3,1,0:T(8,128)(2,1)} fusion(bf16[8,4,512,2,4]{2,4,3,1,0:T(4,128)(2,1)S(1)} %bitcast.244, bf16[8,4,512,128]{2,3,1,0:T(8,128)(2,1)} %fusion.48, s32[8,4,512]{2,1,0:T(4,128)S(1)} %get-tuple-element.10), kind=kOutput, calls=%fused_computation.42.clone.1 | convolution fusion | flops 4370464768 | bytes 12910592 | tf_op jit(solution)/shard_map/abjx,abjvlt->abxvlt/dot_general | solution.py:76
  225.3 18.5 %fusion.35 = bf16[2,4,4,128,1024,1]{4,3,2,0,1,5:T(8,128)(2,1)} fusion(bf16[2,8,128,1024,1,1]{3,2,1,0,5,4:T(8,128)(2,1)S(1)} %bitcast.250, bf16[8,4,128,2,4,128]{5,2,4,3,1,0:T(8,128)(2,1)} %fusion.211), kind=kOutput, calls=%fused_computation.41 | convolution fusion | flops 8589934592 | bytes 20971520 | tf_op jit(solution)/shard_map/vaxj,abxvlt->vbljt/dot_general | solution.py:79
  243.7 15.4 %multiply_reduce_fusion.2 = (f32[]{:T(128)}, f32[2,4,1024,512]{3,2,1,0:T(8,128)}) fusion(bf16[2,4,128,512,1]{3,2,1,4,0:T(8,128)(2,1)S(1)} %bitcast.235, f32[2,4,1024,512,1]{3,2,4,1,0:T(8,128)} %get-tuple-element.19, f32[]{:T(128)S(6)} %neg.4, bf16[2,4,4,128,1024,1]{4,3,2,0,1,5:T(8,128)(2,1)} %fusion.35), kind=kOutput, calls=%fused_computation.15 | convolution fusion | flops 4311744512 | bytes 42991624 | tf_op jit(solution)/shard_map/vbljt,vbtk->vljk/dot_general | solution.py:82
  259.2 22.3 %convert_bitcast_fusion = bf16[2,8,4,4,128,128]{5,4,2,1,3,0:T(8,128)(2,1)} fusion(bf16[2,4,128,512,1,1]{3,2,1,5,4,0:T(8,128)(2,1)S(1)} %bitcast.237, bf16[2,8,128,1024,1]{3,2,1,4,0:T(8,128)(2,1)} %bitcast.248, f32[2,4,1024,512]{3,2,1,0:T(8,128)} %get-tuple-element.21), kind=kOutput, calls=%fused_computation.38 | convolution fusion | flops 12897484800 | bytes 30408704 | tf_op jit(solution)/shard_map/vlaxm,vbtm->vablxt/dot_general | solution.py:88
  281.5 12.1 %multiply_reduce_fusion = bf16[8,4,512,2,4]{2,4,3,1,0:T(4,128)(2,1)S(1)} fusion(bf16[8,4,512,128]{2,3,1,0:T(8,128)(2,1)} %fusion.48, bf16[2,8,4,4,128,128]{5,4,2,1,3,0:T(8,128)(2,1)} %convert_bitcast_fusion, s32[8,4,512]{2,1,0:T(4,128)S(1)} %get-tuple-element.10), kind=kOutput, calls=%fused_computation | convolution fusion | flops 4347265024 | bytes 12910592 | tf_op jit(solution)/shard_map/abjx,vablxt->abjvlt/dot_general | solution.py:91
  293.6 0.2 copy.109
  293.8 12.8 %all_to_all.27 = bf16[2,32,4,512]{3,0,2,1:T(2,128)(2,1)S(1)} all-to-all(bf16[2,32,4,512]{3,0,2,1:T(2,128)(2,1)S(1)} %copy.109), channel_id=1, replica_groups=mesh['gx'=8,'gy'=4] {'gx','gy'}, dimensions={1} | all-to-all | bytes 524288 | tf_op jit(solution)/shard_map/all_to_all | solution.py:95
  306.6 0.2 copy.110
  306.8 1.4 fusion.145
  308.2 1.2 pad_maximum_fusion.1
  309.5 41.5 %psum.15 = f32[2]{0:T(128)S(1)} all-reduce(f32[2]{0:T(128)S(1)} %pad_maximum_fusion.1), channel_id=1, replica_groups=mesh['gx'=8,'gy'=4] {'gx','gy'}, use_global_device_ids=true, to_apply=%region_9.10 | all-reduce | flops 2 | bytes 16 | tf_op jit(solution)/shard_map/psum | solution.py:101
  351.0 0.6 fusion.182
  353.6 11.0 %add_convert_fusion = bf16[2,8,4,4,128,128]{5,4,2,1,3,0:T(8,128)(2,1)} fusion(bf16[2,8,4,4,128,128]{5,4,2,1,3,0:T(8,128)(2,1)} %convert_bitcast_fusion, bf16[2,8,4,4,128,128]{5,4,2,1,3,0:T(8,128)(2,1)} %convert_bitcast_fusion.1, f32[]{:T(128)S(6)} %neg.10, f32[]{:T(128)S(6)} %neg.4), kind=kLoop, calls=%fused_computation.13 | loop fusion | flops 25165824 | bytes 25165832 | tf_op jit(solution)/shard_map/convert_element_type | solution.py:108
  364.6 10.3 %copy.112 = bf16[2,32,4,128,128]{4,3,2,0,1:T(8,128)(2,1)} copy(bf16[2,32,4,128,128]{4,3,1,2,0:T(8,128)(2,1)} %bitcast.238) | data formatting | bytes 16777216 | tf_op jit(solution)/shard_map/reshape | solution.py:108
  375.0 3.6 all-to-all-start.4
  378.6 5.6 convolution_convert_fusion
  384.2 17.6 %multiply_add_fusion = f32[2,4,1024,512]{3,2,1,0:T(8,128)} fusion(f32[2,4,1024,512]{3,2,1,0:T(8,128)} %get-tuple-element.21, f32[2,4,1024,512,1]{3,2,4,1,0:T(8,128)} %get-tuple-element.19, f32[]{:T(128)S(6)} %neg.10, f32[]{:T(128)S(6)} %neg.4), kind=kLoop, calls=%fused_computation.14 | loop fusion | flops 12582912 | bytes 50331656 | tf_op jit(solution)/shard_map/add | solution.py:105
  401.8 158.0 %all-to-all-done.4 = bf16[2,32,4,128,128]{4,3,2,0,1:T(8,128)(2,1)} async-done(((bf16[2,32,4,128,128]{4,3,2,0,1:T(8,128)(2,1)}), bf16[2,32,4,128,128]{4,3,2,0,1:T(8,128)(2,1)}, u32[]{:S(2)}, u32[]{:S(2)}) %all-to-all-start.4) | async-done | bytes 8388640 | tf_op jit(solution)/shard_map/all_to_all | solution.py:109
  559.8 10.5 %copy.113 = bf16[2,32,4,128,128]{4,3,2,1,0:T(8,128)(2,1)} copy(bf16[2,32,4,128,128]{4,3,2,0,1:T(8,128)(2,1)} %all-to-all-done.4) | data formatting | bytes 16777216 | tf_op jit(solution)/shard_map/all_to_all | solution.py:109
  570.3 13.8 %copy.115 = bf16[2,128,128,128]{1,2,3,0:T(8,128)(2,1)} copy(bf16[2,128,128,128]{3,2,1,0:T(8,128)(2,1)} %bitcast.239) | data formatting | bytes 16777216 | tf_op jit(solution)/shard_map/reshape | solution.py:110
  584.1 20.2 %fusion.49 = f32[2,128,128,128]{1,2,3,0:T(8,128)} fusion(bf16[2,128,128,128]{1,2,3,0:T(8,128)(2,1)} %copy.115, bf16[128,2,128,128]{3,0,2,1:T(8,128)(2,1)} %convolution_convert_fusion), kind=kOutput, calls=%fused_computation.52 | convolution fusion | flops 1073741824 | bytes 33554432 | tf_op jit(solution)/shard_map/tvlm,vmxt->vlxt/dot_general | solution.py:111
  604.3 18.2 %copy.117 = f32[2,128,128,128]{3,2,1,0:T(8,128)} copy(f32[2,128,128,128]{1,2,3,0:T(8,128)} %fusion.49) | data formatting | bytes 33554432
  (26 shorter events, 0.7 us)
Async XLA Ops:
  0.6 84.4 %copy-start = (bf16[2,512,512]{2,1,0:T(8,128)(2,1)S(1)}, bf16[2,512,512]{2,1,0:T(8,128)(2,1)}, u32[]{:S(2)}) copy-start(bf16[2,512,512]{2,1,0:T(8,128)(2,1)} %param.13) | copy-start | bytes 3145732
  9.5 43.4 %all-to-all-start = ((bf16[2,32,4,512]{3,2,0,1:T(4,128)(2,1)}), bf16[2,32,4,512]{3,2,0,1:T(4,128)(2,1)S(1)}, u32[]{:S(2)}, u32[]{:S(2)}) async-start(bf16[2,32,4,512]{3,2,0,1:T(4,128)(2,1)} %copy.83), calls=%async_computation | async-start | bytes 524288 | tf_op jit(solution)/shard_map/all_to_all | solution.py:51
  52.9 13.7 %copy-start.5 = (bf16[2,1024,1024]{2,1,0:T(8,128)(2,1)S(1)}, bf16[2,1024,1024]{2,1,0:T(8,128)(2,1)}, u32[]{:S(2)}) copy-start(bf16[2,1024,1024]{2,1,0:T(8,128)(2,1)} %param.12) | copy-start | bytes 12582916
  119.4 31.2 %copy-start.2 = (bf16[8,2,128,128]{3,2,1,0:T(8,128)(2,1)S(1)}, bf16[8,2,128,128]{3,2,1,0:T(8,128)(2,1)}, u32[]{:S(2)}) copy-start(bf16[8,2,128,128]{3,2,1,0:T(8,128)(2,1)} %param.11) | copy-start | bytes 1572868
  119.4 31.2 %copy-start.7 = (f32[2,128]{1,0:T(2,128)S(1)}, f32[2,128]{1,0:T(2,128)}, u32[]{:S(2)}) copy-start(f32[2,128]{1,0:T(2,128)} %param.9) | copy-start | bytes 3076
  119.4 77.7 %copy-start.3 = (s32[512]{0:T(512)S(1)}, s32[512]{0:T(512)}, u32[]{:S(2)}) copy-start(s32[512]{0:T(512)} %param.8) | copy-start | bytes 6148
  211.5 13.7 %copy-start.6 = (bf16[2,1024,1024]{2,1,0:T(8,128)(2,1)S(1)}, bf16[2,1024,1024]{2,1,0:T(8,128)(2,1)}, u32[]{:S(2)}) copy-start(bf16[2,1024,1024]{2,1,0:T(8,128)(2,1)} %param.12) | copy-start | bytes 12582916
  374.9 3.6 copy-start.4
  375.0 184.8 %all-to-all-start.4 = ((bf16[2,32,4,128,128]{4,3,2,0,1:T(8,128)(2,1)}), bf16[2,32,4,128,128]{4,3,2,0,1:T(8,128)(2,1)}, u32[]{:S(2)}, u32[]{:S(2)}) async-start(bf16[2,32,4,128,128]{4,3,2,0,1:T(8,128)(2,1)} %copy.112), calls=%async_computation.4 | async-start | bytes 16777216 | tf_op jit(solution)/shard_map/all_to_all | solution.py:109
  604.3 18.2 %copy-start.1 = (bf16[2,512,512]{2,1,0:T(8,128)(2,1)S(1)}, bf16[2,512,512]{2,1,0:T(8,128)(2,1)}, u32[]{:S(2)}) copy-start(bf16[2,512,512]{2,1,0:T(8,128)(2,1)} %param.13) | copy-start | bytes 3145732
